TPU v7x, 256 devices: a whole 4x4x8 slice. The times are simulated.
256 devices in a mesh: group: 16 (over z, core), member: 16 (over x, y).
Axes of the slice: x: 4, y: 4, z: 8, core: 2. Of those that a mesh axis runs over, the one named last changes fastest.
Arguments:
- embeddings: bfloat16 [32, 8192, 768], P('group', 'member')
- counts: int32 [32], replicated, may hold values from 1 to 8192, as said below
Outputs:
- best_cosine: float32 [32, 8192], P('group', 'member')
Inputs may be any that keep to these rules, and one draw needn't show every extreme that they name: Cluster c holds rows 0 to counts[c] - 1 of its 8192 slots; the rest are padding; some cluster fills all 8192 slots and some cluster holds a single row.
All inputs are finite; a program needn't handle non-finite values.
Results may differ from a plain program's by a relative error of at most 0.0003.
Values may be sent and summed in bfloat16 or wider, within the bound.
A program may use at most 128 MiB of HBM per device.

v0:
```python
import jax
import jax.numpy as jnp
from jax import lax
from jax.sharding import PartitionSpec as P


def tile_best(carry, unit, piece, start, mine, pos):
    width = piece.shape[1]
    cols = start + jnp.arange(width, dtype=jnp.int32)
    scores = jnp.einsum("crd,cnd->crn", unit, piece, preferred_element_type=jnp.float32)
    usable = (cols[None, None, :] < mine[:, None, None]) & (
        cols[None, None, :] != pos[None, :, None]
    )
    return jnp.maximum(carry, jnp.max(jnp.where(usable, scores, -jnp.inf), axis=2))


def fold_piece(carry, unit, piece, mine, pos):
    width = piece.shape[1]
    block = 1024
    blocks = jnp.moveaxis(
        piece.reshape(piece.shape[0], width // block, block, piece.shape[2]), 1, 0
    )

    def step(inner, item):
        index, part_rows = item
        return (tile_best(inner, unit, part_rows, index * block, mine, pos), None)

    steps_idx = jnp.arange(width // block, dtype=jnp.int32)
    result, unused = lax.scan(step, carry, (steps_idx, blocks))
    return result


def shards(embeddings, counts):
    clusters, rows, width = embeddings.shape
    first = lax.axis_index("group") * clusters
    mine = lax.dynamic_slice_in_dim(counts, first, clusters)
    member_idx = lax.axis_index("member")
    offset = member_idx * rows
    pos = offset + jnp.arange(rows, dtype=jnp.int32)
    valid = pos[None, :] < mine[:, None]
    local_sum = jnp.einsum(
        "cr,crd->d", valid.astype(jnp.bfloat16), embeddings, preferred_element_type=jnp.float32
    )
    total = lax.psum(local_sum, ("group", "member"))
    mean = total / jnp.sum(counts).astype(jnp.float32)
    centered = embeddings.astype(jnp.float32) - mean
    unit = (
        centered * lax.rsqrt(jnp.sum(centered * centered, axis=2, keepdims=True) + 1e-06)
    ).astype(jnp.bfloat16)
    start_best = jnp.full((clusters, rows), -1.0, jnp.float32)
    best = fold_piece(
        start_best, unit, lax.all_gather(unit, "member", axis=1, tiled=True), mine, pos
    )
    return jnp.where(valid, best, jnp.float32(-1.0))


def solution(mesh):
    return jax.shard_map(
        shards,
        mesh=mesh,
        in_specs=(P("group", "member", None), P()),
        out_specs=P("group", "member"),
        check_vma=False,
    )
```

profile of v0, /device:TPU:1, one launch (start us, length us, event | category | flops | bytes accessed | tf_op | source)
XLA Modules:
  0.0 323.6 jit_solution(12125064556257797177)
XLA Ops:
  6.5 1.4 reduce_sum.18
  8.0 0.7 dynamic_slice.11
  8.8 1.7 convolution_reduce_fusion
  10.5 81.4 %psum.7 = f32[768]{0:T(1024)S(1)} all-reduce(f32[768]{0:T(1024)S(1)} %convolution_reduce_fusion), channel_id=1, replica_groups=mesh['group'=16,'member'=16] {'group','member'}, use_global_device_ids=true, to_apply=%region_0.0 | all-reduce | flops 768 | bytes 6144 | tf_op jit(solution)/shard_map/psum | solution.py:44
  92.6 1.9 multiply_reduce_fusion
  94.5 1.6 multiply_convert_fusion
  96.1 154.5 %all-gather.2.cloned.1.call-done = bf16[2,8192,768]{2,1,0:T(8,128)(2,1)} async-done(((bf16[2,512,768]{2,1,0:T(8,128)(2,1)}), bf16[2,8192,768]{2,1,0:T(8,128)(2,1)}) %all-gather.2.cloned.1.call-update) | async-done | bytes 25165840 | tf_op jit(solution)/shard_map/all_gather | solution.py:52
  250.6 21.0 %copy.8 = bf16[2,8,1024,768]{3,2,0,1:T(8,128)(2,1)} copy(bf16[2,8,1024,768]{3,2,1,0:T(8,128)(2,1)} %bitcast.27) | data formatting | bytes 50331648 | tf_op jit(solution)/shard_map/reshape | solution.py:21
  271.6 44.5 %while.11 = (s32[]{:T(128)}, f32[2,512]{1,0:T(2,128)S(1)}, s32[8]{0:T(128)S(1)}, s32[2]{0:T(128)S(1)}, bf16[8,2,1024,768]{3,2,1,0:T(8,128)(2,1)}, /*index=5*/bf1...) while((s32[]{:T(128)}, f32[2,512]{1,0:T(2,128)S(1)}, ...), condition=%wide.region_5.6_spmd.clone, body=%wide.region_3.5_spmd.clone.sunk | while | flops 1614287360 | bytes 5804695 | solution.py:29
  273.3 3.8 %fusion.17 = f32[2,512]{1,0:T(2,128)S(1)} fusion(pred[512,1024]{0,1:T(8,128)(4,1)S(1)} %broadcast_compare_fusion.4, pred[2,1024]{1,0:T(4,128)(4,1)S(1)} %broadcast_compare_fusion.5, bf16[2,512,768]{2,1,0:T(8,128)(2,1)S(1)} %get-tuple-element.152, bf16[8,2,1024,768]{3,2,1,0:T(8,128)(2,1)} %get-tuple-element.151, s32[]{:T(128)} %get-tuple-element.137), kind=kOutput, calls=%fused_computation.2.clone.1 | convolution fusion | flops 1613757440 | bytes 5249536 | tf_op jit(solution)/shard_map/while/body/eval_jaxpr/crd,cnd->crn/dot_general | solution.py:10
  277.2 0.6 dynamic_slice.23
  278.8 3.8 %fusion.17 = f32[2,512]{1,0:T(2,128)S(1)} fusion(pred[512,1024]{0,1:T(8,128)(4,1)S(1)} %broadcast_compare_fusion.4, pred[2,1024]{1,0:T(4,128)(4,1)S(1)} %broadcast_compare_fusion.5, bf16[2,512,768]{2,1,0:T(8,128)(2,1)S(1)} %get-tuple-element.152, bf16[8,2,1024,768]{3,2,1,0:T(8,128)(2,1)} %get-tuple-element.151, s32[]{:T(128)} %get-tuple-element.137), kind=kOutput, calls=%fused_computation.2.clone.1 | convolution fusion | flops 1613757440 | bytes 5249536 | tf_op jit(solution)/shard_map/while/body/eval_jaxpr/crd,cnd->crn/dot_general | solution.py:10
  282.7 0.6 dynamic_slice.23
  284.4 3.8 %fusion.17 = f32[2,512]{1,0:T(2,128)S(1)} fusion(pred[512,1024]{0,1:T(8,128)(4,1)S(1)} %broadcast_compare_fusion.4, pred[2,1024]{1,0:T(4,128)(4,1)S(1)} %broadcast_compare_fusion.5, bf16[2,512,768]{2,1,0:T(8,128)(2,1)S(1)} %get-tuple-element.152, bf16[8,2,1024,768]{3,2,1,0:T(8,128)(2,1)} %get-tuple-element.151, s32[]{:T(128)} %get-tuple-element.137), kind=kOutput, calls=%fused_computation.2.clone.1 | convolution fusion | flops 1613757440 | bytes 5249536 | tf_op jit(solution)/shard_map/while/body/eval_jaxpr/crd,cnd->crn/dot_general | solution.py:10
  288.3 0.6 dynamic_slice.23
  290.0 3.8 %fusion.17 = f32[2,512]{1,0:T(2,128)S(1)} fusion(pred[512,1024]{0,1:T(8,128)(4,1)S(1)} %broadcast_compare_fusion.4, pred[2,1024]{1,0:T(4,128)(4,1)S(1)} %broadcast_compare_fusion.5, bf16[2,512,768]{2,1,0:T(8,128)(2,1)S(1)} %get-tuple-element.152, bf16[8,2,1024,768]{3,2,1,0:T(8,128)(2,1)} %get-tuple-element.151, s32[]{:T(128)} %get-tuple-element.137), kind=kOutput, calls=%fused_computation.2.clone.1 | convolution fusion | flops 1613757440 | bytes 5249536 | tf_op jit(solution)/shard_map/while/body/eval_jaxpr/crd,cnd->crn/dot_general | solution.py:10
  293.9 0.6 dynamic_slice.23
  295.5 3.8 %fusion.17 = f32[2,512]{1,0:T(2,128)S(1)} fusion(pred[512,1024]{0,1:T(8,128)(4,1)S(1)} %broadcast_compare_fusion.4, pred[2,1024]{1,0:T(4,128)(4,1)S(1)} %broadcast_compare_fusion.5, bf16[2,512,768]{2,1,0:T(8,128)(2,1)S(1)} %get-tuple-element.152, bf16[8,2,1024,768]{3,2,1,0:T(8,128)(2,1)} %get-tuple-element.151, s32[]{:T(128)} %get-tuple-element.137), kind=kOutput, calls=%fused_computation.2.clone.1 | convolution fusion | flops 1613757440 | bytes 5249536 | tf_op jit(solution)/shard_map/while/body/eval_jaxpr/crd,cnd->crn/dot_general | solution.py:10
  299.4 0.6 dynamic_slice.23
  301.1 3.8 %fusion.17 = f32[2,512]{1,0:T(2,128)S(1)} fusion(pred[512,1024]{0,1:T(8,128)(4,1)S(1)} %broadcast_compare_fusion.4, pred[2,1024]{1,0:T(4,128)(4,1)S(1)} %broadcast_compare_fusion.5, bf16[2,512,768]{2,1,0:T(8,128)(2,1)S(1)} %get-tuple-element.152, bf16[8,2,1024,768]{3,2,1,0:T(8,128)(2,1)} %get-tuple-element.151, s32[]{:T(128)} %get-tuple-element.137), kind=kOutput, calls=%fused_computation.2.clone.1 | convolution fusion | flops 1613757440 | bytes 5249536 | tf_op jit(solution)/shard_map/while/body/eval_jaxpr/crd,cnd->crn/dot_general | solution.py:10
  305.0 0.6 dynamic_slice.23
  306.7 3.8 %fusion.17 = f32[2,512]{1,0:T(2,128)S(1)} fusion(pred[512,1024]{0,1:T(8,128)(4,1)S(1)} %broadcast_compare_fusion.4, pred[2,1024]{1,0:T(4,128)(4,1)S(1)} %broadcast_compare_fusion.5, bf16[2,512,768]{2,1,0:T(8,128)(2,1)S(1)} %get-tuple-element.152, bf16[8,2,1024,768]{3,2,1,0:T(8,128)(2,1)} %get-tuple-element.151, s32[]{:T(128)} %get-tuple-element.137), kind=kOutput, calls=%fused_computation.2.clone.1 | convolution fusion | flops 1613757440 | bytes 5249536 | tf_op jit(solution)/shard_map/while/body/eval_jaxpr/crd,cnd->crn/dot_general | solution.py:10
  312.2 3.8 %fusion.17 = f32[2,512]{1,0:T(2,128)S(1)} fusion(pred[512,1024]{0,1:T(8,128)(4,1)S(1)} %broadcast_compare_fusion.4, pred[2,1024]{1,0:T(4,128)(4,1)S(1)} %broadcast_compare_fusion.5, bf16[2,512,768]{2,1,0:T(8,128)(2,1)S(1)} %get-tuple-element.152, bf16[8,2,1024,768]{3,2,1,0:T(8,128)(2,1)} %get-tuple-element.151, s32[]{:T(128)} %get-tuple-element.137), kind=kOutput, calls=%fused_computation.2.clone.1 | convolution fusion | flops 1613757440 | bytes 5249536 | tf_op jit(solution)/shard_map/while/body/eval_jaxpr/crd,cnd->crn/dot_general | solution.py:10
  316.1 0.7 compare_select_fusion
  (54 shorter events, 5.0 us)
Async XLA Ops:
  6.5 88.0 %copy-start = (bf16[2,512,768]{2,1,0:T(8,128)(2,1)S(1)}, bf16[2,512,768]{2,1,0:T(8,128)(2,1)}, u32[]{:S(2)}) copy-start(bf16[2,512,768]{2,1,0:T(8,128)(2,1)} %param.4) | copy-start | bytes 4718596
  6.5 244.1 %all-gather.2.cloned.1.call-start = ((), (), s32[]{:S(2)}) async-start(), calls=%async_computation | async-start | bytes 26738688 | tf_op jit(solution)/shard_map/all_gather | solution.py:52
  250.6 21.0 %copy-start.1 = (bf16[2,512,768]{2,1,0:T(8,128)(2,1)S(1)}, bf16[2,512,768]{2,1,0:T(8,128)(2,1)}, u32[]{:S(2)}) copy-start(bf16[2,512,768]{2,1,0:T(8,128)(2,1)} %multiply_convert_fusion) | copy-start | bytes 4718596
Sparse Core Ops, SparseCore 0:
  96.2 154.3 all-gather.1
where the time goes:
time: 324 us
  waiting for transfers between devices  155 us (48%)
  blocking collectives  81.4 us (25%)
  matrix products  32.4 us (10%)
  local copies, waits for them, and re-layouts  26.5 us (8%)
  between operations  14.1 us (4%)
  other arithmetic  9.3 us (3%)
  loops' own time  5.43 us (2%)
    all_gather x1, waiting for transfers between devices, shards(): lax.all_gather(unit, 'member', axis=1, tiled=True)  155 us
    psum x1, blocking collectives, shards(): total = lax.psum(local_sum, ('group', 'member'))  81.4 us
    dot_general x8, matrix products, tile_best(): jnp.einsum('crd,cnd->crn', unit, piece, preferred_element_type=jnp.float32)  30.6 us
    reshape x1, local copies, waits for them, and re-layouts, fold_piece(): piece.reshape(piece.shape[0], width // block, block, piece.shape[2])  21 us
  transfers between devices with their start and end apart: 1, of which 1 were waited for; matrix products, arithmetic and copies ran while one was open for 0% of the time, Pallas kernels for 0%

commit v1 on v0

v1 whole, which is shorter than its diff:
```python
import jax
import jax.numpy as jnp
from jax import lax
from jax.experimental import pallas as pl
from jax.experimental.pallas import tpu as pltpu
from jax.sharding import PartitionSpec as P

MESH = pl.DeviceIdType.MESH
F32 = jnp.float32
LOW = -4.0
HALF = 256
BLOCK = 512
D = 768


def kernel(
    counts_ref, emb_ref, out_ref,
    yraw, uraw, draw, yu, uu, du, m_y, m_u, c_u, c_d,
    mbx, mby, mbc, mbz, r_y, r_u, r_d, in_y, in_u, in_d,
    xs_sem, y_sem, f_sem, u_sem, d_sem,
    mxs, mxr, mys, myr, mcs, mcr, mzs, mzr,
    rs_sem, iy_sem, iu_sem, id_sem,
):
    g = lax.axis_index("group")
    m = lax.axis_index("member")
    z, k = g // 2, g % 2
    x, y = m // 4, m % 4
    up, down = (y + 1) % 4, (y + 3) % 4
    half_d = (k + y // 2) % 2

    def dev(zz, kk, xx, yy):
        return (2 * zz + kk, 4 * xx + yy)

    def remote(src, dst, ssem, rsem, device):
        return pltpu.make_async_remote_copy(
            src_ref=src, dst_ref=dst, send_sem=ssem, recv_sem=rsem,
            device_id=device, device_id_type=MESH,
        )

    def recv(ref, sem):
        remote(ref, ref, sem, sem, dev(z, 1 - k, x, y)).wait_recv()

    barrier = pltpu.get_barrier_semaphore()

    def greet_plane(i, c):
        other = (16 * k + m + 1 + i) % 32
        pl.semaphore_signal(
            barrier, inc=1, device_id=(2 * z + other // 16, other % 16), device_id_type=MESH
        )
        return c

    def greet_z(i, c):
        pl.semaphore_signal(
            barrier, inc=1, device_id=(2 * ((z + 1 + i) % 8) + k, m), device_id_type=MESH
        )
        return c

    lax.fori_loop(0, 31, greet_plane, 0)
    lax.fori_loop(0, 7, greet_z, 0)

    total = jnp.zeros((8, D), F32)
    for s in range(2):
        left = counts_ref[4 * z + 2 * k + s] - BLOCK * m

        def add_rows(i, acc, s=s, left=left):
            rows = emb_ref[s, pl.ds(pl.multiple_of(i * 64, 64), 64), :].astype(F32)
            at = lax.broadcasted_iota(jnp.int32, (64, D), 0) + i * 64
            rows = jnp.where(at < left, rows, 0.0)
            return acc + jnp.sum(rows.reshape(8, 8, D), axis=0)

        total = lax.fori_loop(0, BLOCK // 64, add_rows, total)
    mbx[x] = total

    pl.semaphore_wait(barrier, 38)

    s_odd = (x + 1) % 2
    s_even = x % 2
    j_odd = 2 * k + s_odd
    j_even = 2 * k + s_even
    p_odd = jnp.where((x + 4 - j_odd) % 4 == 1, 1, 2)
    here = j_even == x

    def send_odd(h):
        return remote(
            emb_ref.at[s_odd, pl.ds(h * HALF, HALF)], yraw.at[p_odd, h],
            xs_sem.at[0, h], y_sem.at[p_odd, h], dev(z, h, j_odd, y),
        )

    def send_even(h, p):
        return remote(
            emb_ref.at[s_even, pl.ds(h * HALF, HALF)], yraw.at[p, h],
            xs_sem.at[1, h], y_sem.at[p, h], dev(z, h, j_even, y),
        )

    for h in range(2):
        @pl.when(here & (k == h))
        def _(h=h):
            pltpu.make_async_copy(
                emb_ref.at[s_even, pl.ds(h * HALF, HALF)], yraw.at[0, h], y_sem.at[0, h]
            ).start()

        @pl.when(here & (k != h))
        def _(h=h):
            send_even(h, 0).start()

    def exchange(buf, size, mine, ssem, rsem, device):
        def go(i, c):
            to = (mine + 1 + i) % size
            remote(buf.at[mine], buf.at[mine], ssem.at[i], rsem.at[mine], device(to)).start()
            return c

        lax.fori_loop(0, size - 1, go, 0)

    def collect(buf, size, mine, ssem, rsem, device):
        def done(i, c):
            frm = (mine + 1 + i) % size
            copy = remote(buf.at[mine], buf.at[frm], ssem.at[i], rsem.at[frm], device(frm))
            copy.wait_recv()
            copy.wait_send()
            return c

        lax.fori_loop(0, size - 1, done, 0)
        acc = buf[0]
        for i in range(1, size):
            acc = acc + buf[i]
        return acc

    on_x = lambda i: dev(z, k, i, y)
    on_y = lambda i: dev(z, k, x, i)
    on_c = lambda i: dev(z, i, x, y)
    on_z = lambda i: dev(i, k, x, y)

    exchange(mbx, 4, x, mxs, mxr, on_x)
    for h in range(2):
        send_odd(h).start()

    def forwards(p):
        src = yraw.at[p, k]
        return (
            remote(src, uraw.at[p], f_sem.at[p, 0], u_sem.at[p], dev(z, k, x, down)),
            remote(src, draw.at[p], f_sem.at[p, 1], d_sem.at[p],
                   dev(z, (k + up // 2) % 2, x, up)),
            remote(src, yraw.at[p, k], f_sem.at[p, 2], y_sem.at[p, k], dev(z, 1 - k, x, y)),
        )

    def arrive(p):
        recv(yraw.at[p, k], y_sem.at[p, k])
        for copy in forwards(p):
            copy.start()

    arrive(0)
    mby[y] = collect(mbx, 4, x, mxs, mxr, on_x)
    exchange(mby, 4, y, mys, myr, on_y)
    mbc[k] = collect(mby, 4, y, mys, myr, on_y)
    exchange(mbc, 2, k, mcs, mcr, on_c)
    mbz[z] = collect(mbc, 2, k, mcs, mcr, on_c)
    exchange(mbz, 8, z, mzs, mzr, on_z)
    summed = collect(mbz, 8, z, mzs, mzr, on_z)
    rows_all = counts_ref[0]
    for i in range(1, 32):
        rows_all = rows_all + counts_ref[i]
    mean = jnp.sum(summed, axis=0, keepdims=True) / rows_all.astype(F32)

    arrive(1)
    arrive(2)
    for h in range(2):
        send_odd(h).wait_send()

        @pl.when(j_even != x)
        def _(h=h):
            send_even(h, 3).start()

    n_home = counts_ref[4 * z + x]

    def origin(p):
        d = p + jnp.where(p == 2, 1, 0) - jnp.where(p == 3, 1, 0)
        return (x + d) % 4

    def left_y(p):
        return n_home - BLOCK * (4 * origin(p) + y)

    def left_u(p):
        return n_home - BLOCK * (4 * origin(p) + up) - HALF * k

    def left_d(p):
        return n_home - BLOCK * (4 * origin(p) + down) - HALF * half_d

    def normalise(src, dst):
        def step(i, c):
            at = pl.ds(pl.multiple_of(i * 32, 32), 32)
            v = src[at, :].astype(F32) - mean
            q = jnp.sum(v * v, axis=1, keepdims=True)
            dst[at, :] = (v * lax.rsqrt(q + 1e-06)).astype(jnp.bfloat16)
            return c

        lax.fori_loop(0, HALF // 32, step, 0)

    def scores(a, b):
        return lax.dot_general(
            a, b, (((1,), (1,)), ((), ())), preferred_element_type=F32
        )

    def bias(left):
        at = lax.broadcasted_iota(jnp.int32, (1, HALF), 1)
        return jnp.where(at < left, 0.0, LOW)

    def fold_lanes(sc):
        return jnp.maximum(sc[:, :128], sc[:, 128:])

    def fold_rows(sc):
        return jnp.max(sc.reshape(sc.shape[0] // 8, 8, sc.shape[1]), axis=0)

    def mask_rows(sc, left):
        at = lax.broadcasted_iota(jnp.int32, sc.shape, 0)
        return jnp.where(at < left, sc, LOW)

    def y_block(p):
        return yu[p].reshape(BLOCK, D)

    def own_tile(pr, pc):
        sc = scores(y_block(pr), yu[pc, k]) + bias(left_y(pc) - HALF * k)
        row = lax.broadcasted_iota(jnp.int32, sc.shape, 0)
        col = lax.broadcasted_iota(jnp.int32, sc.shape, 1) + HALF * k
        col = col + jnp.where(pr == pc, 0, BLOCK)
        sc = jnp.where(row == col, LOW, sc)
        m_y[pr] = jnp.maximum(m_y[pr], fold_lanes(sc))

    def up_tile(py, pu):
        sc = scores(y_block(py), uu[pu])
        m_y[py] = jnp.maximum(m_y[py], fold_lanes(sc + bias(left_u(pu))))
        c_u[pu] = jnp.maximum(c_u[pu], fold_rows(mask_rows(sc, left_y(py))))

    def cross_tile(pu, pd):
        sc = scores(uu[pu], du[pd])
        m_u[pu] = jnp.maximum(m_u[pu], fold_lanes(sc + bias(left_d(pd))))
        c_d[pd] = jnp.maximum(c_d[pd], fold_rows(mask_rows(sc, left_u(pu))))

    def loop(n, body):
        def step(i, c):
            body(i)
            return c

        lax.fori_loop(0, n, step, 0)

    def ready_y(p):
        normalise(yraw.at[p, k], yu.at[p, k])
        recv(yraw.at[p, 1 - k], y_sem.at[p, 1 - k])
        normalise(yraw.at[p, 1 - k], yu.at[p, 1 - k])

    def ready_ud(p, n_y):
        recv(uraw.at[p], u_sem.at[p])
        normalise(uraw.at[p], uu.at[p])
        loop(n_y, lambda py: up_tile(py, p))
        recv(draw.at[p], d_sem.at[p])
        normalise(draw.at[p], du.at[p])
        loop(p + 1, lambda pu: cross_tile(pu, p))
        loop(p, lambda pd: cross_tile(p, pd))

    m_y[...] = jnp.full(m_y.shape, LOW, F32)
    m_u[...] = jnp.full(m_u.shape, LOW, F32)
    c_u[...] = jnp.full(c_u.shape, LOW, F32)
    c_d[...] = jnp.full(c_d.shape, LOW, F32)

    loop(3, ready_y)
    loop(9, lambda i: own_tile(i // 3, i % 3))
    loop(2, lambda p: ready_ud(p, 3))
    arrive(3)
    ready_y(3)
    loop(4, lambda p: own_tile(p, 3))
    loop(3, lambda p: own_tile(3, p))
    loop(2, lambda p: up_tile(3, p))
    loop(2, lambda p: ready_ud(2 + p, 4))

    def flat(v):
        return jnp.max(v.T, axis=0, keepdims=True)

    s_home = x % 2
    k_home = x // 2

    def result_copies(p):
        xx = origin(p)
        return (
            remote(r_y.at[p], in_y.at[s_home, k], rs_sem.at[p, 0], iy_sem.at[s_home, k],
                   dev(z, k_home, xx, y)),
            remote(r_u.at[p], in_u.at[s_home, k], rs_sem.at[p, 1], iu_sem.at[s_home, k],
                   dev(z, k_home, xx, up)),
            remote(r_d.at[p], in_d.at[s_home, half_d], rs_sem.at[p, 2],
                   id_sem.at[s_home, half_d], dev(z, k_home, xx, down)),
        )

    mine = k == k_home
    for p in range(4):
        r_u[p] = jnp.maximum(flat(m_u[p]), jnp.max(c_u[p], axis=0, keepdims=True))
        r_d[p] = jnp.max(c_d[p], axis=0, keepdims=True)
        r_y[p] = flat(m_y[p])
        copies = result_copies(p)
        copies[1].start()
        copies[2].start()
        if p == 0:
            @pl.when(mine)
            def _():
                pltpu.make_async_copy(
                    r_y.at[0], in_y.at[s_home, k], iy_sem.at[s_home, k]
                ).start()

            @pl.when(jnp.logical_not(mine))
            def _():
                result_copies(0)[0].start()
        else:
            copies[0].start()

    for s in range(2):
        for h in range(2):
            recv(in_y.at[s, h], iy_sem.at[s, h])
            recv(in_u.at[s, h], iu_sem.at[s, h])
            recv(in_d.at[s, h], id_sem.at[s, h])
        best = jnp.maximum(in_y[s, 0], in_y[s, 1])
        both = jnp.concatenate(
            [jnp.maximum(in_u[s, h], in_d[s, h]) for h in range(2)], axis=1
        )
        best = jnp.maximum(jnp.maximum(best, both), -1.0)
        at = lax.broadcasted_iota(jnp.int32, (1, BLOCK), 1) + BLOCK * m
        n = counts_ref[4 * z + 2 * k + s]
        out_ref[s : s + 1, :] = jnp.where(at < n, best, -1.0)

    for h in range(2):
        @pl.when(here & (k != h))
        def _(h=h):
            send_even(h, 0).wait_send()

        @pl.when(j_even != x)
        def _(h=h):
            send_even(h, 3).wait_send()

    def finish(p):
        for copy in forwards(p):
            copy.wait_send()
        copies = result_copies(p)
        copies[1].wait_send()
        copies[2].wait_send()

        @pl.when((p > 0) | jnp.logical_not(mine))
        def _():
            result_copies(p)[0].wait_send()

    loop(4, finish)


def shards(embeddings, counts):
    dma = pltpu.SemaphoreType.DMA
    bf = jnp.bfloat16
    return pl.pallas_call(
        kernel,
        out_shape=jax.ShapeDtypeStruct((2, BLOCK), F32),
        in_specs=[
            pl.BlockSpec(memory_space=pltpu.SMEM),
            pl.BlockSpec(memory_space=pltpu.VMEM),
        ],
        out_specs=pl.BlockSpec(memory_space=pltpu.VMEM),
        scratch_shapes=[
            pltpu.VMEM((4, 2, HALF, D), bf),
            pltpu.VMEM((4, HALF, D), bf),
            pltpu.VMEM((4, HALF, D), bf),
            pltpu.VMEM((4, 2, HALF, D), bf),
            pltpu.VMEM((4, HALF, D), bf),
            pltpu.VMEM((4, HALF, D), bf),
            pltpu.VMEM((4, BLOCK, 128), F32),
            pltpu.VMEM((4, HALF, 128), F32),
            pltpu.VMEM((4, 8, HALF), F32),
            pltpu.VMEM((4, 8, HALF), F32),
            pltpu.VMEM((4, 8, D), F32),
            pltpu.VMEM((4, 8, D), F32),
            pltpu.VMEM((2, 8, D), F32),
            pltpu.VMEM((8, 8, D), F32),
            pltpu.VMEM((4, 1, BLOCK), F32),
            pltpu.VMEM((4, 1, HALF), F32),
            pltpu.VMEM((4, 1, HALF), F32),
            pltpu.VMEM((2, 2, 1, BLOCK), F32),
            pltpu.VMEM((2, 2, 1, HALF), F32),
            pltpu.VMEM((2, 2, 1, HALF), F32),
            dma((2, 2)), dma((4, 2)), dma((4, 3)), dma((4,)), dma((4,)),
            dma((3,)), dma((4,)), dma((3,)), dma((4,)),
            dma((1,)), dma((2,)), dma((7,)), dma((8,)),
            dma((4, 3)), dma((2, 2)), dma((2, 2)), dma((2, 2)),
        ],
        compiler_params=pltpu.CompilerParams(
            collective_id=0, has_side_effects=True, vmem_limit_bytes=48 * 1024 * 1024
        ),
        cost_estimate=pl.CostEstimate(
            flops=8 * 10**9, bytes_accessed=2 * 10**6, transcendentals=0
        ),
    )(counts, embeddings)


def solution(mesh):
    return jax.shard_map(
        shards,
        mesh=mesh,
        in_specs=(P("group", "member", None), P()),
        out_specs=P("group", "member"),
        check_vma=False,
    )
```

time: 324 us -> 73.1 us (0.23)
  waiting for transfers between devices: 155 us -> 0 us
  blocking collectives: 81.4 us -> 0 us
  Pallas kernels: 0 us -> 70.3 us
  matrix products: 32.4 us -> 0 us
  local copies, waits for them, and re-layouts: 26.5 us -> 2.66 us
  between operations: 14.1 us -> 0.01 us
  other arithmetic: 9.3 us -> 0 us
  loops' own time: 5.43 us -> 0 us
    all_gather x1 -> x0, waiting for transfers between devices: 155 us -> none  [shards(): lax.all_gather(unit, 'member', axis=1, tiled=True)]
    psum x1 -> x0, blocking collectives: 81.4 us -> none  [shards(): total = lax.psum(local_sum, ('group', 'member'))]
    pallas_call x0 -> x1, Pallas kernels: none -> 70.3 us  [shards(): pl.pallas_call(kernel, out_shape=jax.ShapeDtypeStruct((2, BLOCK), F32), i...]
    dot_general x9 -> x0, matrix products: 32.4 us -> none  [the longest x8 30.6 us: tile_best(): jnp.einsum('crd,cnd->crn', unit, piece, preferred_element_type=jnp.float32)]
    reshape x1 -> x0, local copies, waits for them, and re-layouts: 21 us -> none  [fold_piece(): piece.reshape(piece.shape[0], width // block, block, piece.shape[2])]
    dynamic_slice x9 -> x0, local copies, waits for them, and re-layouts: 5.5 us -> none  [the longest x8 4.77 us: fold_piece(): result, unused = lax.scan(step, carry, (steps_idx, blocks))]
    another operation x1 -> x0, loops' own time: 5.43 us -> none  [fold_piece(): result, unused = lax.scan(step, carry, (steps_idx, blocks))]
    reduce_sum x2 -> x0, other arithmetic: 3.31 us -> none  [the longest x1 1.9 us: shards(): jnp.sum(centered * centered, axis=2, keepdims=True) + 1e-06]
  transfers between devices with their start and end apart: 1 -> 0, of which waited for: 1 -> 0; matrix products, arithmetic and copies ran while one was open for 0% -> 0% of each run, Pallas kernels for 0% -> 0%
where the time goes in v1:
time: 73.1 us; the launch traced here: 73 us
  Pallas kernels  70.3 us (96%)
  local copies, waits for them, and re-layouts  2.66 us (4%)
    pallas_call x1, Pallas kernels, shards(): pl.pallas_call(kernel, out_shape=jax.ShapeDtypeStruct((2, BLOCK), F32), i...  70.3 us
    unnamed x5, local copies, waits for them, and re-layouts  2.66 us

profile of v1, /device:TPU:1, one launch (start us, length us, event | category | flops | bytes accessed | tf_op | source)
XLA Modules:
  0.0 73.0 jit_solution(1502056187698746001)
XLA Ops:
  0.0 0.0 copy-start
  0.0 1.4 %copy-done = bf16[2,512,768]{2,1,0:T(8,128)(2,1)S(1)} copy-done((bf16[2,512,768]{2,1,0:T(8,128)(2,1)S(1)}, bf16[2,512,768]{2,1,0:T(8,128)(2,1)}, u32[]{:S(2)}) %copy-start) | copy-done | bytes 1572888
  1.4 0.0 copy-start.1
  1.4 0.7 copy-done.1
  2.1 70.3 %shard_map.28 = f32[2,512]{1,0:T(2,128)S(1)} custom-call(s32[32]{0:T(128)S(1)} %copy-done.1, bf16[2,512,768]{2,1,0:T(8,128)(2,1)S(1)} %copy-done), custom_call_target="tpu_custom_call" | custom-call | flops 8000000000 | bytes 2000000 | tf_op jit(solution)/shard_map/pallas_call | solution.py:352
  72.4 0.6 copy.4
Async XLA Ops:
  0.0 1.4 %copy-start = (bf16[2,512,768]{2,1,0:T(8,128)(2,1)S(1)}, bf16[2,512,768]{2,1,0:T(8,128)(2,1)}, u32[]{:S(2)}) copy-start(bf16[2,512,768]{2,1,0:T(8,128)(2,1)} %emb_ref.1) | copy-start | bytes 4718596
  1.4 0.7 copy-start.1

commit v2 on v1

--- a/solution.py
+++ b/solution.py
@@ -14,11 +14,11 @@
 
 
 def kernel(
-    counts_ref, emb_ref, out_ref,
-    yraw, uraw, draw, yu, uu, du, m_y, m_u, c_u, c_d,
-    mbx, mby, mbc, mbz, r_y, r_u, r_d, in_y, in_u, in_d,
-    xs_sem, y_sem, f_sem, u_sem, d_sem,
-    mxs, mxr, mys, myr, mcs, mcr, mzs, mzr,
+    counts_ref, emb_hbm, out_ref,
+    emb_ref, relay, yraw, uraw, draw, yu, uu, du, m_y, m_u, c_u, c_d,
+    mba, mbb, r_y, r_u, r_d, in_y, in_u, in_d,
+    xs_sem, relay_s, relay_r, y_sem, f_sem, u_sem, d_sem,
+    e_sem, as_sem, ar_sem, bs_sem, br_sem,
     rs_sem, iy_sem, iu_sem, id_sem,
 ):
     g = lax.axis_index("group")
@@ -40,6 +40,8 @@
     def recv(ref, sem):
         remote(ref, ref, sem, sem, dev(z, 1 - k, x, y)).wait_recv()
 
+    load = pltpu.make_async_copy(emb_hbm, emb_ref, e_sem)
+    load.start()
     barrier = pltpu.get_barrier_semaphore()
 
     def greet_plane(i, c):
@@ -50,13 +52,15 @@
         return c
 
     def greet_z(i, c):
+        zz = (z + 1 + i // 2) % 8
         pl.semaphore_signal(
-            barrier, inc=1, device_id=(2 * ((z + 1 + i) % 8) + k, m), device_id_type=MESH
+            barrier, inc=1, device_id=(2 * zz + i % 2, m), device_id_type=MESH
         )
         return c
 
     lax.fori_loop(0, 31, greet_plane, 0)
-    lax.fori_loop(0, 7, greet_z, 0)
+    lax.fori_loop(0, 14, greet_z, 0)
+    load.wait()
 
     total = jnp.zeros((8, D), F32)
     for s in range(2):
@@ -69,9 +73,9 @@
             return acc + jnp.sum(rows.reshape(8, 8, D), axis=0)
 
         total = lax.fori_loop(0, BLOCK // 64, add_rows, total)
-    mbx[x] = total
-
-    pl.semaphore_wait(barrier, 38)
+    mba[m] = jnp.sum(total, axis=0, keepdims=True)
+
+    pl.semaphore_wait(barrier, 45)
 
     s_odd = (x + 1) % 2
     s_even = x % 2
@@ -86,10 +90,21 @@
             xs_sem.at[0, h], y_sem.at[p_odd, h], dev(z, h, j_odd, y),
         )
 
-    def send_even(h, p):
+    def send_own(h):
         return remote(
-            emb_ref.at[s_even, pl.ds(h * HALF, HALF)], yraw.at[p, h],
-            xs_sem.at[1, h], y_sem.at[p, h], dev(z, h, j_even, y),
+            emb_ref.at[s_even, pl.ds(h * HALF, HALF)], yraw.at[0, h],
+            xs_sem.at[1, h], y_sem.at[0, h], dev(z, h, x, y),
+        )
+
+    def send_far(h):
+        return remote(
+            emb_ref.at[s_even, pl.ds(h * HALF, HALF)], relay,
+            xs_sem.at[1, h], relay_r, dev(z, h, (x + 1 + 2 * h) % 4, y),
+        )
+
+    def pass_on():
+        return remote(
+            relay, yraw.at[3, k], relay_s, y_sem.at[3, k], dev(z, k, (x + 1 + 2 * k) % 4, y)
         )
 
     for h in range(2):
@@ -101,36 +116,22 @@
 
         @pl.when(here & (k != h))
         def _(h=h):
-            send_even(h, 0).start()
-
-    def exchange(buf, size, mine, ssem, rsem, device):
+            send_own(h).start()
+
+    def exchange(buf, mine, ssem, rsem, device):
         def go(i, c):
-            to = (mine + 1 + i) % size
-            remote(buf.at[mine], buf.at[mine], ssem.at[i], rsem.at[mine], device(to)).start()
+            remote(buf.at[mine], buf.at[mine], ssem, rsem, device((mine + 1 + i) % 16)).start()
             return c
 
-        lax.fori_loop(0, size - 1, go, 0)
-
-    def collect(buf, size, mine, ssem, rsem, device):
-        def done(i, c):
-            frm = (mine + 1 + i) % size
-            copy = remote(buf.at[mine], buf.at[frm], ssem.at[i], rsem.at[frm], device(frm))
-            copy.wait_recv()
-            copy.wait_send()
-            return c
-
-        lax.fori_loop(0, size - 1, done, 0)
-        acc = buf[0]
-        for i in range(1, size):
-            acc = acc + buf[i]
-        return acc
-
-    on_x = lambda i: dev(z, k, i, y)
-    on_y = lambda i: dev(z, k, x, i)
-    on_c = lambda i: dev(z, i, x, y)
-    on_z = lambda i: dev(i, k, x, y)
-
-    exchange(mbx, 4, x, mxs, mxr, on_x)
+        lax.fori_loop(0, 15, go, 0)
+
+    def collect(buf, ssem, rsem):
+        copy = remote(buf.at[:15], buf.at[:15], ssem, rsem, dev(z, 1 - k, x, y))
+        copy.wait_recv()
+        copy.wait_send()
+        return jnp.sum(buf[...], axis=0)
+
+    exchange(mba, m, as_sem, ar_sem, lambda i: (g, i))
     for h in range(2):
         send_odd(h).start()
 
@@ -149,26 +150,21 @@
             copy.start()
 
     arrive(0)
-    mby[y] = collect(mbx, 4, x, mxs, mxr, on_x)
-    exchange(mby, 4, y, mys, myr, on_y)
-    mbc[k] = collect(mby, 4, y, mys, myr, on_y)
-    exchange(mbc, 2, k, mcs, mcr, on_c)
-    mbz[z] = collect(mbc, 2, k, mcs, mcr, on_c)
-    exchange(mbz, 8, z, mzs, mzr, on_z)
-    summed = collect(mbz, 8, z, mzs, mzr, on_z)
+    mbb[g] = collect(mba, as_sem, ar_sem)
+    exchange(mbb, g, bs_sem, br_sem, lambda i: (i, m))
+    arrive(1)
+    for h in range(2):
+        send_odd(h).wait_send()
+
+        @pl.when(j_even != x)
+        def _(h=h):
+            send_far(h).start()
+
+    summed = collect(mbb, bs_sem, br_sem)
     rows_all = counts_ref[0]
     for i in range(1, 32):
         rows_all = rows_all + counts_ref[i]
-    mean = jnp.sum(summed, axis=0, keepdims=True) / rows_all.astype(F32)
-
-    arrive(1)
-    arrive(2)
-    for h in range(2):
-        send_odd(h).wait_send()
-
-        @pl.when(j_even != x)
-        def _(h=h):
-            send_even(h, 3).start()
+    mean = summed / rows_all.astype(F32)
 
     n_home = counts_ref[4 * z + x]
 
@@ -187,13 +183,13 @@
 
     def normalise(src, dst):
         def step(i, c):
-            at = pl.ds(pl.multiple_of(i * 32, 32), 32)
+            at = pl.ds(pl.multiple_of(i * 128, 128), 128)
             v = src[at, :].astype(F32) - mean
             q = jnp.sum(v * v, axis=1, keepdims=True)
             dst[at, :] = (v * lax.rsqrt(q + 1e-06)).astype(jnp.bfloat16)
             return c
 
-        lax.fori_loop(0, HALF // 32, step, 0)
+        lax.fori_loop(0, HALF // 128, step, 0, unroll=2)
 
     def scores(a, b):
         return lax.dot_general(
@@ -235,41 +231,56 @@
         m_u[pu] = jnp.maximum(m_u[pu], fold_lanes(sc + bias(left_d(pd))))
         c_d[pd] = jnp.maximum(c_d[pd], fold_rows(mask_rows(sc, left_u(pu))))
 
-    def loop(n, body):
+    def loop(n, body, unroll=1):
         def step(i, c):
             body(i)
             return c
 
-        lax.fori_loop(0, n, step, 0)
+        lax.fori_loop(0, n, step, 0, unroll=unroll)
 
     def ready_y(p):
         normalise(yraw.at[p, k], yu.at[p, k])
         recv(yraw.at[p, 1 - k], y_sem.at[p, 1 - k])
         normalise(yraw.at[p, 1 - k], yu.at[p, 1 - k])
 
-    def ready_ud(p, n_y):
+    def ready_u(p, n_y):
         recv(uraw.at[p], u_sem.at[p])
         normalise(uraw.at[p], uu.at[p])
-        loop(n_y, lambda py: up_tile(py, p))
+        loop(n_y, lambda py: up_tile(py, p), n_y)
+
+    def ready_d(p):
         recv(draw.at[p], d_sem.at[p])
         normalise(draw.at[p], du.at[p])
-        loop(p + 1, lambda pu: cross_tile(pu, p))
-        loop(p, lambda pd: cross_tile(p, pd))
+        loop(p + 1, lambda pu: cross_tile(pu, p), p + 1)
+        loop(p, lambda pd: cross_tile(p, pd), max(p, 1))
 
     m_y[...] = jnp.full(m_y.shape, LOW, F32)
     m_u[...] = jnp.full(m_u.shape, LOW, F32)
     c_u[...] = jnp.full(c_u.shape, LOW, F32)
     c_d[...] = jnp.full(c_d.shape, LOW, F32)
 
-    loop(3, ready_y)
-    loop(9, lambda i: own_tile(i // 3, i % 3))
-    loop(2, lambda p: ready_ud(p, 3))
+    loop(2, ready_y)
+    loop(4, lambda i: own_tile(i // 2, i % 2), 4)
+    arrive(2)
+    recv(relay, relay_r)
+    pass_on().start()
+    ready_u(0, 2)
+    ready_d(0)
+    ready_y(2)
+    loop(3, lambda p: own_tile(p, 2), 3)
+    loop(2, lambda p: own_tile(2, p), 2)
+    up_tile(2, 0)
+    ready_u(1, 3)
     arrive(3)
+    ready_d(1)
     ready_y(3)
-    loop(4, lambda p: own_tile(p, 3))
-    loop(3, lambda p: own_tile(3, p))
-    loop(2, lambda p: up_tile(3, p))
-    loop(2, lambda p: ready_ud(2 + p, 4))
+    loop(4, lambda p: own_tile(p, 3), 4)
+    loop(3, lambda p: own_tile(3, p), 3)
+    loop(2, lambda p: up_tile(3, p), 2)
+    ready_u(2, 4)
+    ready_d(2)
+    ready_u(3, 4)
+    ready_d(3)
 
     def flat(v):
         return jnp.max(v.T, axis=0, keepdims=True)
@@ -323,14 +334,15 @@
         n = counts_ref[4 * z + 2 * k + s]
         out_ref[s : s + 1, :] = jnp.where(at < n, best, -1.0)
 
+    pass_on().wait_send()
     for h in range(2):
         @pl.when(here & (k != h))
         def _(h=h):
-            send_even(h, 0).wait_send()
+            send_own(h).wait_send()
 
         @pl.when(j_even != x)
         def _(h=h):
-            send_even(h, 3).wait_send()
+            send_far(h).wait_send()
 
     def finish(p):
         for copy in forwards(p):
@@ -354,10 +366,12 @@
         out_shape=jax.ShapeDtypeStruct((2, BLOCK), F32),
         in_specs=[
             pl.BlockSpec(memory_space=pltpu.SMEM),
-            pl.BlockSpec(memory_space=pltpu.VMEM),
+            pl.BlockSpec(memory_space=pl.ANY),
         ],
         out_specs=pl.BlockSpec(memory_space=pltpu.VMEM),
         scratch_shapes=[
+            pltpu.VMEM((2, BLOCK, D), bf),
+            pltpu.VMEM((HALF, D), bf),
             pltpu.VMEM((4, 2, HALF, D), bf),
             pltpu.VMEM((4, HALF, D), bf),
             pltpu.VMEM((4, HALF, D), bf),
@@ -368,19 +382,16 @@
             pltpu.VMEM((4, HALF, 128), F32),
             pltpu.VMEM((4, 8, HALF), F32),
             pltpu.VMEM((4, 8, HALF), F32),
-            pltpu.VMEM((4, 8, D), F32),
-            pltpu.VMEM((4, 8, D), F32),
-            pltpu.VMEM((2, 8, D), F32),
-            pltpu.VMEM((8, 8, D), F32),
+            pltpu.VMEM((16, 1, D), F32),
+            pltpu.VMEM((16, 1, D), F32),
             pltpu.VMEM((4, 1, BLOCK), F32),
             pltpu.VMEM((4, 1, HALF), F32),
             pltpu.VMEM((4, 1, HALF), F32),
             pltpu.VMEM((2, 2, 1, BLOCK), F32),
             pltpu.VMEM((2, 2, 1, HALF), F32),
             pltpu.VMEM((2, 2, 1, HALF), F32),
-            dma((2, 2)), dma((4, 2)), dma((4, 3)), dma((4,)), dma((4,)),
-            dma((3,)), dma((4,)), dma((3,)), dma((4,)),
-            dma((1,)), dma((2,)), dma((7,)), dma((8,)),
+            dma((2, 2)), dma, dma, dma((4, 2)), dma((4, 3)), dma((4,)), dma((4,)),
+            dma, dma, dma, dma, dma,
             dma((4, 3)), dma((2, 2)), dma((2, 2)), dma((2, 2)),
         ],
         compiler_params=pltpu.CompilerParams(

time: 73.1 us -> 58.1 us (0.79)
  Pallas kernels: 70.3 us -> 55.3 us
    pallas_call x1, Pallas kernels: 70.3 us -> 55.3 us  [shards(): pl.pallas_call(kernel, out_shape=jax.ShapeDtypeStruct((2, BLOCK), F32), i...]
where the time goes in v2:
time: 58.1 us; the launch traced here: 58 us
  Pallas kernels  55.3 us (95%)
  local copies, waits for them, and re-layouts  2.66 us (5%)
    pallas_call x1, Pallas kernels, shards(): pl.pallas_call(kernel, out_shape=jax.ShapeDtypeStruct((2, BLOCK), F32), i...  55.3 us
    unnamed x5, local copies, waits for them, and re-layouts  2.66 us

profile of v2, /device:TPU:1, one launch (start us, length us, event | category | flops | bytes accessed | tf_op | source)
XLA Modules:
  0.0 58.0 jit_solution(7236317843450734168)
XLA Ops:
  0.0 0.0 copy-start
  0.0 1.4 %copy-done = bf16[2,512,768]{2,1,0:T(8,128)(2,1)S(1)} copy-done((bf16[2,512,768]{2,1,0:T(8,128)(2,1)S(1)}, bf16[2,512,768]{2,1,0:T(8,128)(2,1)}, u32[]{:S(2)}) %copy-start) | copy-done | bytes 1572888
  1.4 0.0 copy-start.1
  1.4 0.7 %copy-done.1 = s32[32]{0:T(128)S(1)} copy-done((s32[32]{0:T(128)S(1)}, s32[32]{0:T(128)}, u32[]{:S(2)}) %copy-start.1) | copy-done | bytes 152
  2.1 55.3 %shard_map.28 = f32[2,512]{1,0:T(2,128)S(1)} custom-call(s32[32]{0:T(128)S(1)} %copy-done.1, bf16[2,512,768]{2,1,0:T(8,128)(2,1)S(1)} %copy-done), custom_call_target="tpu_custom_call" | custom-call | flops 8000000000 | bytes 2000000 | tf_op jit(solution)/shard_map/pallas_call | solution.py:364
  57.4 0.6 %copy.4 = f32[2,512]{1,0:T(2,128)} copy(f32[2,512]{1,0:T(2,128)S(1)} %shard_map.28) | data formatting | bytes 8192
Async XLA Ops:
  0.0 1.4 %copy-start = (bf16[2,512,768]{2,1,0:T(8,128)(2,1)S(1)}, bf16[2,512,768]{2,1,0:T(8,128)(2,1)}, u32[]{:S(2)}) copy-start(bf16[2,512,768]{2,1,0:T(8,128)(2,1)} %emb_hbm.1) | copy-start | bytes 4718596
  1.4 0.7 %copy-start.1 = (s32[32]{0:T(128)S(1)}, s32[32]{0:T(128)}, u32[]{:S(2)}) copy-start(s32[32]{0:T(128)} %counts_ref.1) | copy-start | bytes 388

commit v3 on v2

--- a/solution.py
+++ b/solution.py
@@ -16,9 +16,9 @@
 def kernel(
     counts_ref, emb_hbm, out_ref,
     emb_ref, relay, yraw, uraw, draw, yu, uu, du, m_y, m_u, c_u, c_d,
-    mba, mbb, r_y, r_u, r_d, in_y, in_u, in_d,
+    m_mine, m_row, m_col, m_pl, m_all, r_y, r_u, r_d, in_y, in_u, in_d,
     xs_sem, relay_s, relay_r, y_sem, f_sem, u_sem, d_sem,
-    e_sem, as_sem, ar_sem, bs_sem, br_sem,
+    e_sem, ms_sem, mr_sem, cs_sem, cr_sem, ps_sem, pr_sem, ma_sem, ml_sem,
     rs_sem, iy_sem, iu_sem, id_sem,
 ):
     g = lax.axis_index("group")
@@ -44,22 +44,24 @@
     load.start()
     barrier = pltpu.get_barrier_semaphore()
 
-    def greet_plane(i, c):
-        other = (16 * k + m + 1 + i) % 32
-        pl.semaphore_signal(
-            barrier, inc=1, device_id=(2 * z + other // 16, other % 16), device_id_type=MESH
-        )
-        return c
-
-    def greet_z(i, c):
-        zz = (z + 1 + i // 2) % 8
-        pl.semaphore_signal(
-            barrier, inc=1, device_id=(2 * zz + i % 2, m), device_id_type=MESH
-        )
-        return c
-
-    lax.fori_loop(0, 31, greet_plane, 0)
-    lax.fori_loop(0, 14, greet_z, 0)
+    chief = (x == 3) & (k == 0)
+
+    def greet(device):
+        pl.semaphore_signal(barrier, inc=1, device_id=device, device_id_type=MESH)
+
+    greet(dev(z, 1 - k, x, y))
+    for kk in range(2):
+        for i in range(1, 4):
+            greet(dev(z, kk, (x + i) % 4, y))
+        greet(dev(z, kk, x, up))
+        greet(dev(z, kk, x, down))
+
+    @pl.when(chief)
+    def _():
+        greet(dev(z, k, x, (y + 2) % 4))
+        for i in range(1, 8):
+            greet(dev((z + i) % 8, k, x, y))
+
     load.wait()
 
     total = jnp.zeros((8, D), F32)
@@ -73,9 +75,25 @@
             return acc + jnp.sum(rows.reshape(8, 8, D), axis=0)
 
         total = lax.fori_loop(0, BLOCK // 64, add_rows, total)
-    mba[m] = jnp.sum(total, axis=0, keepdims=True)
-
-    pl.semaphore_wait(barrier, 45)
+    m_mine[...] = jnp.sum(total, axis=0, keepdims=True)
+
+    @pl.when(chief)
+    def _():
+        pl.semaphore_wait(barrier, 19)
+
+    @pl.when(jnp.logical_not(chief))
+    def _():
+        pl.semaphore_wait(barrier, 11)
+
+
+    row = 4 * k + x
+
+    def to_chief():
+        return remote(m_mine, m_row.at[row], ms_sem, mr_sem, dev(z, 0, 3, y))
+
+    @pl.when(jnp.logical_not(chief))
+    def _():
+        to_chief().start()
 
     s_odd = (x + 1) % 2
     s_even = x % 2
@@ -118,20 +136,22 @@
         def _(h=h):
             send_own(h).start()
 
-    def exchange(buf, mine, ssem, rsem, device):
-        def go(i, c):
-            remote(buf.at[mine], buf.at[mine], ssem, rsem, device((mine + 1 + i) % 16)).start()
-            return c
-
-        lax.fori_loop(0, 15, go, 0)
-
-    def collect(buf, ssem, rsem):
-        copy = remote(buf.at[:15], buf.at[:15], ssem, rsem, dev(z, 1 - k, x, y))
+    def send_mean(i):
+        return remote(m_all, m_all, ma_sem, ml_sem, dev(z, i // 4, i % 4, y))
+
+    def exchange(buf, size, mine, ssem, rsem, device):
+        for i in range(1, size):
+            to = (mine + i) % size
+            remote(buf.at[mine], buf.at[mine], ssem, rsem, device(to)).start()
+
+    def collect(buf, size, ssem, rsem):
+        copy = remote(
+            buf.at[: size - 1], buf.at[: size - 1], ssem, rsem, dev(z, 1 - k, x, y)
+        )
         copy.wait_recv()
         copy.wait_send()
         return jnp.sum(buf[...], axis=0)
 
-    exchange(mba, m, as_sem, ar_sem, lambda i: (g, i))
     for h in range(2):
         send_odd(h).start()
 
@@ -149,9 +169,24 @@
         for copy in forwards(p):
             copy.start()
 
+    @pl.when(chief)
+    def _():
+        m_row[3] = m_mine[...]
+        recv(m_row.at[:7], mr_sem)
+        m_col[y] = jnp.sum(m_row[...], axis=0)
+        exchange(m_col, 4, y, cs_sem, cr_sem, lambda i: dev(z, k, x, i))
+
     arrive(0)
-    mbb[g] = collect(mba, as_sem, ar_sem)
-    exchange(mbb, g, bs_sem, br_sem, lambda i: (i, m))
+
+    @pl.when(chief)
+    def _():
+        m_pl[z] = collect(m_col, 4, cs_sem, cr_sem)
+        exchange(m_pl, 8, z, ps_sem, pr_sem, lambda i: dev(i, k, x, y))
+        m_all[...] = collect(m_pl, 8, ps_sem, pr_sem)
+        for i in range(8):
+            if i != 3:
+                send_mean(i).start()
+
     arrive(1)
     for h in range(2):
         send_odd(h).wait_send()
@@ -160,11 +195,18 @@
         def _(h=h):
             send_far(h).start()
 
-    summed = collect(mbb, bs_sem, br_sem)
+    arrive(2)
+    recv(relay, relay_r)
+    pass_on().start()
+
+    @pl.when(jnp.logical_not(chief))
+    def _():
+        recv(m_all, ml_sem)
+
     rows_all = counts_ref[0]
     for i in range(1, 32):
         rows_all = rows_all + counts_ref[i]
-    mean = summed / rows_all.astype(F32)
+    mean = m_all[...] / rows_all.astype(F32)
 
     n_home = counts_ref[4 * z + x]
 
@@ -261,9 +303,6 @@
 
     loop(2, ready_y)
     loop(4, lambda i: own_tile(i // 2, i % 2), 4)
-    arrive(2)
-    recv(relay, relay_r)
-    pass_on().start()
     ready_u(0, 2)
     ready_d(0)
     ready_y(2)
@@ -333,6 +372,14 @@
         at = lax.broadcasted_iota(jnp.int32, (1, BLOCK), 1) + BLOCK * m
         n = counts_ref[4 * z + 2 * k + s]
         out_ref[s : s + 1, :] = jnp.where(at < n, best, -1.0)
+
+    @pl.when(chief)
+    def _():
+        remote(m_row.at[:7], m_row.at[:7], ma_sem, ma_sem, dev(z, 1 - k, x, y)).wait_send()
+
+    @pl.when(jnp.logical_not(chief))
+    def _():
+        to_chief().wait_send()
 
     pass_on().wait_send()
     for h in range(2):
@@ -382,8 +429,11 @@
             pltpu.VMEM((4, HALF, 128), F32),
             pltpu.VMEM((4, 8, HALF), F32),
             pltpu.VMEM((4, 8, HALF), F32),
-            pltpu.VMEM((16, 1, D), F32),
-            pltpu.VMEM((16, 1, D), F32),
+            pltpu.VMEM((1, D), F32),
+            pltpu.VMEM((8, 1, D), F32),
+            pltpu.VMEM((4, 1, D), F32),
+            pltpu.VMEM((8, 1, D), F32),
+            pltpu.VMEM((1, D), F32),
             pltpu.VMEM((4, 1, BLOCK), F32),
             pltpu.VMEM((4, 1, HALF), F32),
             pltpu.VMEM((4, 1, HALF), F32),
@@ -391,7 +441,7 @@
             pltpu.VMEM((2, 2, 1, HALF), F32),
             pltpu.VMEM((2, 2, 1, HALF), F32),
             dma((2, 2)), dma, dma, dma((4, 2)), dma((4, 3)), dma((4,)), dma((4,)),
-            dma, dma, dma, dma, dma,
+            dma, dma, dma, dma, dma, dma, dma, dma, dma,
             dma((4, 3)), dma((2, 2)), dma((2, 2)), dma((2, 2)),
         ],
         compiler_params=pltpu.CompilerParams(

time: 58.1 us -> 55.6 us (0.957)
  Pallas kernels: 55.3 us -> 52.4 us
    pallas_call x1, Pallas kernels: 55.3 us -> 52.4 us  [shards(): pl.pallas_call(kernel, out_shape=jax.ShapeDtypeStruct((2, BLOCK), F32), i...]
where the time goes in v3:
time: 55.6 us; the launch traced here: 55.1 us
  Pallas kernels  52.4 us (94%)
  local copies, waits for them, and re-layouts  2.66 us (5%)
    pallas_call x1, Pallas kernels, shards(): pl.pallas_call(kernel, out_shape=jax.ShapeDtypeStruct((2, BLOCK), F32), i...  52.4 us
    unnamed x5, local copies, waits for them, and re-layouts  2.66 us

profile of v3, /device:TPU:1, one launch (start us, length us, event | category | flops | bytes accessed | tf_op | source)
XLA Modules:
  0.0 55.1 jit_solution(12897755123658841914)
XLA Ops:
  0.0 0.0 copy-start
  0.0 1.4 %copy-done = bf16[2,512,768]{2,1,0:T(8,128)(2,1)S(1)} copy-done((bf16[2,512,768]{2,1,0:T(8,128)(2,1)S(1)}, bf16[2,512,768]{2,1,0:T(8,128)(2,1)}, u32[]{:S(2)}) %copy-start) | copy-done | bytes 1572888
  1.4 0.0 copy-start.1
  1.4 0.7 %copy-done.1 = s32[32]{0:T(128)S(1)} copy-done((s32[32]{0:T(128)S(1)}, s32[32]{0:T(128)}, u32[]{:S(2)}) %copy-start.1) | copy-done | bytes 152
  2.1 52.4 %shard_map.28 = f32[2,512]{1,0:T(2,128)S(1)} custom-call(s32[32]{0:T(128)S(1)} %copy-done.1, bf16[2,512,768]{2,1,0:T(8,128)(2,1)S(1)} %copy-done), custom_call_target="tpu_custom_call" | custom-call | flops 8000000000 | bytes 2000000 | tf_op jit(solution)/shard_map/pallas_call | solution.py:411
  54.5 0.6 %copy.4 = f32[2,512]{1,0:T(2,128)} copy(f32[2,512]{1,0:T(2,128)S(1)} %shard_map.28) | data formatting | bytes 8192
Async XLA Ops:
  0.0 1.4 %copy-start = (bf16[2,512,768]{2,1,0:T(8,128)(2,1)S(1)}, bf16[2,512,768]{2,1,0:T(8,128)(2,1)}, u32[]{:S(2)}) copy-start(bf16[2,512,768]{2,1,0:T(8,128)(2,1)} %emb_hbm.1) | copy-start | bytes 4718596
  1.4 0.7 %copy-start.1 = (s32[32]{0:T(128)S(1)}, s32[32]{0:T(128)}, u32[]{:S(2)}) copy-start(s32[32]{0:T(128)} %counts_ref.1) | copy-start | bytes 388

commit v4 on v3

--- a/solution.py
+++ b/solution.py
@@ -14,11 +14,11 @@
 
 
 def kernel(
-    counts_ref, emb_hbm, out_ref,
-    emb_ref, relay, yraw, uraw, draw, yu, uu, du, m_y, m_u, c_u, c_d,
+    counts_hbm, emb_hbm, out_ref,
+    counts_ref, emb_ref, relay, yraw, uraw, draw, yu, uu, du, m_y, m_u, c_u, c_d,
     m_mine, m_row, m_col, m_pl, m_all, r_y, r_u, r_d, in_y, in_u, in_d,
     xs_sem, relay_s, relay_r, y_sem, f_sem, u_sem, d_sem,
-    e_sem, ms_sem, mr_sem, cs_sem, cr_sem, ps_sem, pr_sem, ma_sem, ml_sem,
+    e_sem, n_sem, ms_sem, mr_sem, cs_sem, cr_sem, ps_sem, pr_sem, ma_sem, ml_sem,
     rs_sem, iy_sem, iu_sem, id_sem,
 ):
     g = lax.axis_index("group")
@@ -42,6 +42,8 @@
 
     load = pltpu.make_async_copy(emb_hbm, emb_ref, e_sem)
     load.start()
+    sizes = pltpu.make_async_copy(counts_hbm, counts_ref, n_sem)
+    sizes.start()
     barrier = pltpu.get_barrier_semaphore()
 
     chief = (x == 3) & (k == 0)
@@ -62,6 +64,7 @@
         for i in range(1, 8):
             greet(dev((z + i) % 8, k, x, y))
 
+    sizes.wait()
     load.wait()
 
     total = jnp.zeros((8, D), F32)
@@ -412,11 +415,12 @@
         kernel,
         out_shape=jax.ShapeDtypeStruct((2, BLOCK), F32),
         in_specs=[
-            pl.BlockSpec(memory_space=pltpu.SMEM),
+            pl.BlockSpec(memory_space=pl.ANY),
             pl.BlockSpec(memory_space=pl.ANY),
         ],
         out_specs=pl.BlockSpec(memory_space=pltpu.VMEM),
         scratch_shapes=[
+            pltpu.SMEM((32,), jnp.int32),
             pltpu.VMEM((2, BLOCK, D), bf),
             pltpu.VMEM((HALF, D), bf),
             pltpu.VMEM((4, 2, HALF, D), bf),
@@ -441,11 +445,11 @@
             pltpu.VMEM((2, 2, 1, HALF), F32),
             pltpu.VMEM((2, 2, 1, HALF), F32),
             dma((2, 2)), dma, dma, dma((4, 2)), dma((4, 3)), dma((4,)), dma((4,)),
-            dma, dma, dma, dma, dma, dma, dma, dma, dma,
+            dma, dma, dma, dma, dma, dma, dma, dma, dma, dma,
             dma((4, 3)), dma((2, 2)), dma((2, 2)), dma((2, 2)),
         ],
         compiler_params=pltpu.CompilerParams(
-            collective_id=0, has_side_effects=True, vmem_limit_bytes=48 * 1024 * 1024
+            collective_id=0, has_side_effects=True, vmem_limit_bytes=64 * 1024 * 1024
         ),
         cost_estimate=pl.CostEstimate(
             flops=8 * 10**9, bytes_accessed=2 * 10**6, transcendentals=0

time: 55.6 us -> 54.2 us (0.975)
  local copies, waits for them, and re-layouts: 2.66 us -> 1.28 us
    unnamed x5 -> x1, local copies, waits for them, and re-layouts: 2.66 us -> 1.28 us
where the time goes in v4:
time: 54.2 us; the launch traced here: 53.6 us
  Pallas kernels  52.3 us (96%)
  local copies, waits for them, and re-layouts  1.28 us (2%)
    pallas_call x1, Pallas kernels, shards(): pl.pallas_call(kernel, out_shape=jax.ShapeDtypeStruct((2, BLOCK), F32), i...  52.3 us
    unnamed x1, local copies, waits for them, and re-layouts  1.28 us

profile of v4, /device:TPU:1, one launch (start us, length us, event | category | flops | bytes accessed | tf_op | source)
XLA Modules:
  0.0 53.6 jit_solution(3698878280421939343)
XLA Ops:
  0.0 52.3 %shard_map.28 = f32[2,512]{1,0:T(2,128)} custom-call(s32[32]{0:T(128)} %counts_hbm.1, bf16[2,512,768]{2,1,0:T(8,128)(2,1)} %emb_hbm.1), custom_call_target="tpu_custom_call" | custom-call | flops 8000000000 | bytes 2000000 | tf_op jit(solution)/shard_map/pallas_call | solution.py:414
  52.3 1.3 %copy.4 = f32[2,512]{1,0:T(2,128)} copy(f32[2,512]{1,0:T(2,128)} %shard_map.28) | data formatting | bytes 8192

commit v5 on v4

--- a/solution.py
+++ b/solution.py
@@ -158,8 +158,12 @@
     for h in range(2):
         send_odd(h).start()
 
-    def forwards(p):
-        src = yraw.at[p, k]
+    @pl.when(j_even != x)
+    def _():
+        send_far(0).start()
+
+    def forwards(p, src=None):
+        src = yraw.at[p, k] if src is None else src
         return (
             remote(src, uraw.at[p], f_sem.at[p, 0], u_sem.at[p], dev(z, k, x, down)),
             remote(src, draw.at[p], f_sem.at[p, 1], d_sem.at[p],
@@ -172,6 +176,13 @@
         for copy in forwards(p):
             copy.start()
 
+    mine = here & (k == x // 2)
+
+    @pl.when(mine)
+    def _():
+        for copy in forwards(0, emb_ref.at[s_even, pl.ds(pl.multiple_of(k * HALF, HALF), HALF)]):
+            copy.start()
+
     @pl.when(chief)
     def _():
         m_row[3] = m_mine[...]
@@ -179,7 +190,10 @@
         m_col[y] = jnp.sum(m_row[...], axis=0)
         exchange(m_col, 4, y, cs_sem, cr_sem, lambda i: dev(z, k, x, i))
 
-    arrive(0)
+    @pl.when(jnp.logical_not(mine))
+    def _():
+        arrive(0)
+
 
     @pl.when(chief)
     def _():
@@ -190,17 +204,29 @@
             if i != 3:
                 send_mean(i).start()
 
+    @pl.when(k == 0)
+    def _():
+        recv(relay, relay_r)
+        pass_on().start()
+
+    @pl.when(mine)
+    def _():
+        recv(yraw.at[0, k], y_sem.at[0, k])
+
     arrive(1)
     for h in range(2):
         send_odd(h).wait_send()
 
-        @pl.when(j_even != x)
-        def _(h=h):
-            send_far(h).start()
+    @pl.when(j_even != x)
+    def _():
+        send_far(1).start()
 
     arrive(2)
-    recv(relay, relay_r)
-    pass_on().start()
+
+    @pl.when(k == 1)
+    def _():
+        recv(relay, relay_r)
+        pass_on().start()
 
     @pl.when(jnp.logical_not(chief))
     def _():
@@ -312,8 +338,8 @@
     loop(3, lambda p: own_tile(p, 2), 3)
     loop(2, lambda p: own_tile(2, p), 2)
     up_tile(2, 0)
+    arrive(3)
     ready_u(1, 3)
-    arrive(3)
     ready_d(1)
     ready_y(3)
     loop(4, lambda p: own_tile(p, 3), 4)
@@ -321,8 +347,16 @@
     loop(2, lambda p: up_tile(3, p), 2)
     ready_u(2, 4)
     ready_d(2)
-    ready_u(3, 4)
-    ready_d(3)
+    recv(uraw.at[3], u_sem.at[3])
+    recv(draw.at[3], d_sem.at[3])
+    normalise(uraw.at[3], uu.at[3])
+    normalise(draw.at[3], du.at[3])
+    for p in range(4):
+        up_tile(p, 3)
+    for p in range(4):
+        cross_tile(p, 3)
+    for p in range(3):
+        cross_tile(3, p)
 
     def flat(v):
         return jnp.max(v.T, axis=0, keepdims=True)
@@ -341,7 +375,6 @@
                    id_sem.at[s_home, half_d], dev(z, k_home, xx, down)),
         )
 
-    mine = k == k_home
     for p in range(4):
         r_u[p] = jnp.maximum(flat(m_u[p]), jnp.max(c_u[p], axis=0, keepdims=True))
         r_d[p] = jnp.max(c_d[p], axis=0, keepdims=True)

time: 54.2 us -> 53 us (0.978)
  Pallas kernels: 52.3 us -> 51.2 us
    pallas_call x1, Pallas kernels: 52.3 us -> 51.2 us  [shards(): pl.pallas_call(kernel, out_shape=jax.ShapeDtypeStruct((2, BLOCK), F32), i...]
where the time goes in v5:
time: 53 us; the launch traced here: 52.5 us
  Pallas kernels  51.2 us (97%)
  local copies, waits for them, and re-layouts  1.28 us (2%)
    pallas_call x1, Pallas kernels, shards(): pl.pallas_call(kernel, out_shape=jax.ShapeDtypeStruct((2, BLOCK), F32), i...  51.2 us
    unnamed x1, local copies, waits for them, and re-layouts  1.28 us

profile of v5, /device:TPU:1, one launch (start us, length us, event | category | flops | bytes accessed | tf_op | source)
XLA Modules:
  0.0 52.5 jit_solution(17274211841320878147)
XLA Ops:
  0.0 51.2 %shard_map.28 = f32[2,512]{1,0:T(2,128)} custom-call(s32[32]{0:T(128)} %counts_hbm.1, bf16[2,512,768]{2,1,0:T(8,128)(2,1)} %emb_hbm.1), custom_call_target="tpu_custom_call" | custom-call | flops 8000000000 | bytes 2000000 | tf_op jit(solution)/shard_map/pallas_call | solution.py:447
  51.3 1.3 %copy.4 = f32[2,512]{1,0:T(2,128)} copy(f32[2,512]{1,0:T(2,128)} %shard_map.28) | data formatting | bytes 8192

commit v6 on v5

--- a/solution.py
+++ b/solution.py
@@ -296,6 +296,11 @@
         sc = scores(y_block(py), uu[pu])
         m_y[py] = jnp.maximum(m_y[py], fold_lanes(sc + bias(left_u(pu))))
         c_u[pu] = jnp.maximum(c_u[pu], fold_rows(mask_rows(sc, left_y(py))))
+
+    def down_tile(pd):
+        sc = scores(y_block(3), du[pd])
+        m_y[3] = jnp.maximum(m_y[3], fold_lanes(sc + bias(left_d(pd))))
+        c_d[pd] = jnp.maximum(c_d[pd], fold_rows(mask_rows(sc, left_y(3))))
 
     def cross_tile(pu, pd):
         sc = scores(uu[pu], du[pd])
@@ -347,16 +352,8 @@
     loop(2, lambda p: up_tile(3, p), 2)
     ready_u(2, 4)
     ready_d(2)
-    recv(uraw.at[3], u_sem.at[3])
-    recv(draw.at[3], d_sem.at[3])
-    normalise(uraw.at[3], uu.at[3])
-    normalise(draw.at[3], du.at[3])
-    for p in range(4):
-        up_tile(p, 3)
-    for p in range(4):
-        cross_tile(p, 3)
     for p in range(3):
-        cross_tile(3, p)
+        down_tile(p)
 
     def flat(v):
         return jnp.max(v.T, axis=0, keepdims=True)
@@ -375,13 +372,8 @@
                    id_sem.at[s_home, half_d], dev(z, k_home, xx, down)),
         )
 
-    for p in range(4):
-        r_u[p] = jnp.maximum(flat(m_u[p]), jnp.max(c_u[p], axis=0, keepdims=True))
-        r_d[p] = jnp.max(c_d[p], axis=0, keepdims=True)
+    for p in range(3):
         r_y[p] = flat(m_y[p])
-        copies = result_copies(p)
-        copies[1].start()
-        copies[2].start()
         if p == 0:
             @pl.when(mine)
             def _():
@@ -393,7 +385,24 @@
             def _():
                 result_copies(0)[0].start()
         else:
-            copies[0].start()
+            result_copies(p)[0].start()
+
+    recv(uraw.at[3], u_sem.at[3])
+    recv(draw.at[3], d_sem.at[3])
+    normalise(uraw.at[3], uu.at[3])
+    normalise(draw.at[3], du.at[3])
+    up_tile(3, 3)
+    for p in range(4):
+        cross_tile(p, 3)
+    for p in range(3):
+        cross_tile(3, p)
+    r_y[3] = flat(m_y[3])
+    result_copies(3)[0].start()
+    for p in range(4):
+        r_u[p] = jnp.maximum(flat(m_u[p]), jnp.max(c_u[p], axis=0, keepdims=True))
+        r_d[p] = jnp.max(c_d[p], axis=0, keepdims=True)
+        result_copies(p)[1].start()
+        result_copies(p)[2].start()
 
     for s in range(2):
         for h in range(2):
@@ -430,9 +439,8 @@
     def finish(p):
         for copy in forwards(p):
             copy.wait_send()
-        copies = result_copies(p)
-        copies[1].wait_send()
-        copies[2].wait_send()
+        result_copies(p)[1].wait_send()
+        result_copies(p)[2].wait_send()
 
         @pl.when((p > 0) | jnp.logical_not(mine))
         def _():

time: 53 us -> 52.2 us (0.985)
  Pallas kernels: 51.2 us -> 50.5 us
    pallas_call x1, Pallas kernels: 51.2 us -> 50.5 us  [shards(): pl.pallas_call(kernel, out_shape=jax.ShapeDtypeStruct((2, BLOCK), F32), i...]
where the time goes in v6:
time: 52.2 us; the launch traced here: 51.8 us
  Pallas kernels  50.5 us (97%)
  local copies, waits for them, and re-layouts  1.28 us (2%)
    pallas_call x1, Pallas kernels, shards(): pl.pallas_call(kernel, out_shape=jax.ShapeDtypeStruct((2, BLOCK), F32), i...  50.5 us
    unnamed x1, local copies, waits for them, and re-layouts  1.28 us

profile of v6, /device:TPU:1, one launch (start us, length us, event | category | flops | bytes accessed | tf_op | source)
XLA Modules:
  0.0 51.8 jit_solution(13270992885909583867)
XLA Ops:
  0.0 50.5 %shard_map.28 = f32[2,512]{1,0:T(2,128)} custom-call(s32[32]{0:T(128)} %counts_hbm.1, bf16[2,512,768]{2,1,0:T(8,128)(2,1)} %emb_hbm.1), custom_call_target="tpu_custom_call" | custom-call | flops 8000000000 | bytes 2000000 | tf_op jit(solution)/shard_map/pallas_call | solution.py:455
  50.5 1.3 %copy.4 = f32[2,512]{1,0:T(2,128)} copy(f32[2,512]{1,0:T(2,128)} %shard_map.28) | data formatting | bytes 8192

commit v7 on v6

--- a/solution.py
+++ b/solution.py
@@ -267,9 +267,9 @@
             a, b, (((1,), (1,)), ((), ())), preferred_element_type=F32
         )
 
-    def bias(left):
-        at = lax.broadcasted_iota(jnp.int32, (1, HALF), 1)
-        return jnp.where(at < left, 0.0, LOW)
+    def mask_cols(sc, left):
+        at = lax.broadcasted_iota(jnp.int32, sc.shape, 1)
+        return jnp.where(at < left, sc, LOW)
 
     def fold_lanes(sc):
         return jnp.maximum(sc[:, :128], sc[:, 128:])
@@ -285,7 +285,7 @@
         return yu[p].reshape(BLOCK, D)
 
     def own_tile(pr, pc):
-        sc = scores(y_block(pr), yu[pc, k]) + bias(left_y(pc) - HALF * k)
+        sc = mask_cols(scores(y_block(pr), yu[pc, k]), left_y(pc) - HALF * k)
         row = lax.broadcasted_iota(jnp.int32, sc.shape, 0)
         col = lax.broadcasted_iota(jnp.int32, sc.shape, 1) + HALF * k
         col = col + jnp.where(pr == pc, 0, BLOCK)
@@ -294,17 +294,17 @@
 
     def up_tile(py, pu):
         sc = scores(y_block(py), uu[pu])
-        m_y[py] = jnp.maximum(m_y[py], fold_lanes(sc + bias(left_u(pu))))
+        m_y[py] = jnp.maximum(m_y[py], fold_lanes(mask_cols(sc, left_u(pu))))
         c_u[pu] = jnp.maximum(c_u[pu], fold_rows(mask_rows(sc, left_y(py))))
 
     def down_tile(pd):
         sc = scores(y_block(3), du[pd])
-        m_y[3] = jnp.maximum(m_y[3], fold_lanes(sc + bias(left_d(pd))))
+        m_y[3] = jnp.maximum(m_y[3], fold_lanes(mask_cols(sc, left_d(pd))))
         c_d[pd] = jnp.maximum(c_d[pd], fold_rows(mask_rows(sc, left_y(3))))
 
     def cross_tile(pu, pd):
         sc = scores(uu[pu], du[pd])
-        m_u[pu] = jnp.maximum(m_u[pu], fold_lanes(sc + bias(left_d(pd))))
+        m_u[pu] = jnp.maximum(m_u[pu], fold_lanes(mask_cols(sc, left_d(pd))))
         c_d[pd] = jnp.maximum(c_d[pd], fold_rows(mask_rows(sc, left_u(pu))))
 
     def loop(n, body, unroll=1):
@@ -392,8 +392,11 @@
     normalise(uraw.at[3], uu.at[3])
     normalise(draw.at[3], du.at[3])
     up_tile(3, 3)
+    all_u = scores(uu[...].reshape(4 * HALF, D), du[3])
     for p in range(4):
-        cross_tile(p, 3)
+        sc = all_u[p * HALF : (p + 1) * HALF]
+        m_u[p] = jnp.maximum(m_u[p], fold_lanes(mask_cols(sc, left_d(3))))
+        c_d[3] = jnp.maximum(c_d[3], fold_rows(mask_rows(sc, left_u(p))))
     for p in range(3):
         cross_tile(3, p)
     r_y[3] = flat(m_y[3])

time: 52.2 us -> 52.2 us (level)
  no operation moved by 1% of the time
where the time goes in v7:
time: 52.2 us; the launch traced here: 51.8 us
  Pallas kernels  50.5 us (97%)
  local copies, waits for them, and re-layouts  1.28 us (2%)
    pallas_call x1, Pallas kernels, shards(): pl.pallas_call(kernel, out_shape=jax.ShapeDtypeStruct((2, BLOCK), F32), i...  50.5 us
    unnamed x1, local copies, waits for them, and re-layouts  1.28 us

profile of v7, /device:TPU:1, one launch (start us, length us, event | category | flops | bytes accessed | tf_op | source)
XLA Modules:
  0.0 51.8 jit_solution(10658103758030318531)
XLA Ops:
  0.0 50.5 %shard_map.28 = f32[2,512]{1,0:T(2,128)} custom-call(s32[32]{0:T(128)} %counts_hbm.1, bf16[2,512,768]{2,1,0:T(8,128)(2,1)} %emb_hbm.1), custom_call_target="tpu_custom_call" | custom-call | flops 8000000000 | bytes 2000000 | tf_op jit(solution)/shard_map/pallas_call | solution.py:458
  50.5 1.3 %copy.4 = f32[2,512]{1,0:T(2,128)} copy(f32[2,512]{1,0:T(2,128)} %shard_map.28) | data formatting | bytes 8192

commit v8 on v7

--- a/solution.py
+++ b/solution.py
@@ -214,6 +214,7 @@
         recv(yraw.at[0, k], y_sem.at[0, k])
 
     arrive(1)
+    arrive(2)
     for h in range(2):
         send_odd(h).wait_send()
 
@@ -221,7 +222,6 @@
     def _():
         send_far(1).start()
 
-    arrive(2)
 
     @pl.when(k == 1)
     def _():

time: 52.2 us -> 52.2 us (level)
  no operation moved by 1% of the time
where the time goes in v8:
time: 52.2 us; the launch traced here: 51.7 us
  Pallas kernels  50.5 us (97%)
  local copies, waits for them, and re-layouts  1.28 us (2%)
    pallas_call x1, Pallas kernels, shards(): pl.pallas_call(kernel, out_shape=jax.ShapeDtypeStruct((2, BLOCK), F32), i...  50.5 us
    unnamed x1, local copies, waits for them, and re-layouts  1.28 us

profile of v8, /device:TPU:1, one launch (start us, length us, event | category | flops | bytes accessed | tf_op | source)
XLA Modules:
  0.0 51.7 jit_solution(5699226108326640798)
XLA Ops:
  0.0 50.5 %shard_map.28 = f32[2,512]{1,0:T(2,128)} custom-call(s32[32]{0:T(128)} %counts_hbm.1, bf16[2,512,768]{2,1,0:T(8,128)(2,1)} %emb_hbm.1), custom_call_target="tpu_custom_call" | custom-call | flops 8000000000 | bytes 2000000 | tf_op jit(solution)/shard_map/pallas_call | solution.py:458
  50.5 1.3 %copy.4 = f32[2,512]{1,0:T(2,128)} copy(f32[2,512]{1,0:T(2,128)} %shard_map.28) | data formatting | bytes 8192
